TPU v7x, 32 devices: a whole 2x2x4 slice. The times are simulated.
32 devices in a mesh: win: 2 (over x), tm: 16 (over z, y, core).
Axes of the slice: x: 2, y: 2, z: 4, core: 2. Of those that a mesh axis runs over, the one named last changes fastest.
Arguments:
- samples: bfloat16 [16384, 512], P(('win', 'tm')), parts along dimension 0, may hold values from -6 to 6
- block_pairs: int32 [10, 2], replicated, may hold values from 0 to 3, as said below
Outputs:
- lag_values: float32 [2560, 128, 384], P(('win', 'tm')), parts along dimension 0
- amplitude: float32 [2048, 512], P(('win', 'tm')), parts along dimension 0
There are 2 independent parts, one for each index of `win`. A program takes and returns all parts, laid end to end along the dimension named above; an argument that names none is the same for every part. Nothing has to cross between parts.
Inputs may be any that keep to these rules, and one draw needn't show every extreme that they name: `block_pairs`: every pair (a, b) of blocks with a <= b <= a + 3 and b < 4 appears exactly once, as a row (a, b); the order of the rows is drawn.
All inputs are finite; a program needn't handle non-finite values.
Results may differ from a plain program's by a relative error of at most 0.0061.
Values may be sent and summed in bfloat16 or wider, within the bound.
A program may use at most 320 MiB of HBM per device.

v0:
```python
import math

import jax
import jax.numpy as jnp
from jax import lax
from jax.sharding import PartitionSpec as P

NBIN = 1024
SEG = 2048
GROUP = 4
BLK = 128
SMOOTH = 8
LAGS = 384


def with_halo(cells, sides, width):
    for axis, dim in sides:
        count = lax.axis_size(axis)
        ends = count - 1
        head = lax.slice_in_dim(cells, 0, width, axis=dim)
        tail = lax.slice_in_dim(cells, cells.shape[dim] - width, cells.shape[dim], axis=dim)
        cells = jnp.concatenate(
            [
                lax.ppermute(tail, axis, [(i, (i + 1) % count) for i in range(ends)]),
                cells,
                lax.ppermute(head, axis, [((i + 1) % count, i) for i in range(ends)]),
            ],
            axis=dim,
        )
    return cells


def forward_table(first_time, time_count, seg_length, bin_total):
    sample_times = first_time + jnp.arange(time_count, dtype=jnp.int32)
    bin_index = jnp.arange(bin_total, dtype=jnp.int32)
    phases = (sample_times[:, None] * bin_index[None, :] % seg_length).astype(jnp.float32) * (
        2.0 * math.pi / seg_length
    )
    return jnp.concatenate([jnp.cos(phases), -jnp.sin(phases)], axis=1).astype(jnp.bfloat16)


def inverse_table(bin_total, seg_length, lag_total):
    bin_index = jnp.arange(bin_total, dtype=jnp.int32)
    lag_offsets = jnp.arange(lag_total, dtype=jnp.int32) - lag_total // 2
    phases = (bin_index[:, None] * lag_offsets[None, :] % seg_length).astype(jnp.float32) * (
        2.0 * math.pi / seg_length
    )
    return jnp.stack([jnp.cos(phases), -jnp.sin(phases)], axis=1).astype(jnp.bfloat16)


def time_contract(forward_rows, records):
    return lax.dot_general(
        forward_rows, records, (((0,), (0,)), ((), ())), preferred_element_type=jnp.float32
    )


def per_device(samples, block_pairs):
    devices = lax.axis_size("tm")
    position = lax.axis_index("tm")
    shard_len, channels = samples.shape
    seg_count = devices // GROUP
    bin_count = NBIN // devices
    member = position % GROUP
    forward_rows = forward_table(member * shard_len, shard_len, SEG, NBIN)
    partial_value = time_contract(forward_rows, samples) * (1.0 / math.sqrt(SEG))
    arrived = lax.all_to_all(
        partial_value.reshape(2, NBIN, 1, channels), "tm", split_axis=1, concat_axis=2, tiled=True
    )
    spectra = jnp.sum(arrived.reshape(2, bin_count, seg_count, GROUP, channels), axis=3)
    magnitude = jnp.sqrt(spectra[0] * spectra[0] + spectra[1] * spectra[1])
    column = jnp.sum(magnitude, axis=1)
    extended = with_halo(column, (("tm", 0),), SMOOTH)
    window = extended[0:bin_count]
    for offset_bin in range(1, 2 * SMOOTH + 1):
        window = window + extended[offset_bin : offset_bin + bin_count]
    amplitude = window / float((2 * SMOOTH + 1) * seg_count) + 1e-06
    whitened = (spectra / amplitude[None, :, None, :]).astype(jnp.bfloat16)
    pair_total = block_pairs.shape[0]
    blocks = whitened.reshape(2, bin_count, seg_count, channels // BLK, BLK)
    left_side = jnp.take(blocks, block_pairs[:, 0], axis=3)
    right_side = jnp.take(blocks, block_pairs[:, 1], axis=3)
    real_part = jnp.einsum(
        "fspu,fspv->fpuv", left_side[0], right_side[0], preferred_element_type=jnp.float32
    ) + jnp.einsum(
        "fspu,fspv->fpuv", left_side[1], right_side[1], preferred_element_type=jnp.float32
    )
    imag_part = jnp.einsum(
        "fspu,fspv->fpuv", left_side[1], right_side[0], preferred_element_type=jnp.float32
    ) - jnp.einsum(
        "fspu,fspv->fpuv", left_side[0], right_side[1], preferred_element_type=jnp.float32
    )
    cross_spec = (jnp.stack([real_part, imag_part], axis=3) / float(seg_count)).astype(jnp.bfloat16)
    cross_spec = cross_spec.reshape(bin_count, pair_total * BLK, 2, BLK)
    inverse_rows = inverse_table(NBIN, SEG, LAGS)
    lag_values = lax.dot_general(
        lax.all_to_all(cross_spec, "tm", split_axis=1, concat_axis=0, tiled=True),
        inverse_rows,
        (((0, 2), (0, 1)), ((), ())),
        preferred_element_type=jnp.float32,
    ) * (1.0 / math.sqrt(NBIN))
    return (lag_values, amplitude)


def solution(mesh):
    placed = (P(("win", "tm"), None), P())
    return jax.shard_map(
        per_device,
        mesh=mesh,
        in_specs=placed,
        out_specs=(P(("win", "tm"), None, None), P(("win", "tm"), None)),
        check_vma=False,
    )
```

profile of v0, /device:TPU:19, one launch (start us, length us, event | category | flops | bytes accessed | tf_op | source)
XLA Modules:
  0.0 1415.2 jit_solution(17512393614778664957)
XLA Ops:
  0.6 0.0 copy-start
  0.7 9.0 cosine_convert_fusion
  9.7 0.0 copy-done
  9.7 1.3 convolution_multiply_fusion
  11.0 5.2 copy.38
  16.3 0.0 copy-start.3
  16.3 6.6 all-to-all-start
  22.9 0.0 copy-done.3
  23.0 92.1 %all-to-all-done = f32[2,1024,1,512]{3,0,2,1:T(2,128)} async-done(((f32[2,1024,1,512]{3,0,2,1:T(2,128)}), f32[2,1024,1,512]{3,0,2,1:T(2,128)}, u32[]{:S(2)}, u32[]{:S(2)}) %all-to-all-start) | async-done | bytes 4194336 | tf_op jit(solution)/shard_map/all_to_all | solution.py:66
  115.1 4.3 reduce_sum.20
  119.4 0.8 fusion.64
  120.2 0.2 fusion.27
  120.4 2.0 collective-permute-start
  122.5 2.9 collective-permute-start.1
  125.3 1.0 reshape.160
  126.4 0.0 collective-permute-done
  126.4 1.1 collective-permute-done.1
  127.5 0.2 fusion.34
  127.7 0.0 copy-start.2
  127.7 0.6 copy-done.2
  128.4 0.2 fusion.24
  128.6 1.9 gather_fusion
  130.5 1.8 gather_fusion.1
  132.4 4.6 fusion.22
  137.0 14.9 %fusion.28 = f32[64,10,128,128]{3,2,1,0:T(8,128)} fusion(bf16[2,64,4,10,128]{4,2,3,1,0:T(4,128)(2,1)S(1)} %get-tuple-element.18, bf16[2,64,4,10,128]{4,2,3,1,0:T(4,128)(2,1)S(1)} %get-tuple-element.17), kind=kOutput, calls=%fused_computation.53 | convolution fusion | flops 83886080 | bytes 43253760 | tf_op jit(solution)/shard_map/fspu,fspv->fpuv/dot_general | solution.py:82
  151.9 14.9 %fusion.29 = f32[64,10,128,128]{3,2,1,0:T(8,128)} fusion(bf16[2,64,4,10,128]{4,2,3,1,0:T(4,128)(2,1)S(1)} %get-tuple-element.17, bf16[2,64,4,10,128]{4,2,3,1,0:T(4,128)(2,1)S(1)} %get-tuple-element.18), kind=kOutput, calls=%fused_computation.54 | convolution fusion | flops 83886080 | bytes 43253760 | tf_op jit(solution)/shard_map/fspu,fspv->fpuv/dot_general | solution.py:87
  166.8 26.4 %convolution_add_fusion = f32[64,10,128,128]{3,2,1,0:T(8,128)} fusion(f32[64,10,128,128]{3,2,1,0:T(8,128)} %fusion.28, bf16[2,64,4,10,128]{4,2,3,1,0:T(4,128)(2,1)S(1)} %get-tuple-element.18, bf16[2,64,4,10,128]{4,2,3,1,0:T(4,128)(2,1)S(1)} %get-tuple-element.17), kind=kOutput, calls=%fused_computation.7 | convolution fusion | flops 94371840 | bytes 85196800 | tf_op jit(solution)/shard_map/fspu,fspv->fpuv/dot_general | solution.py:84
  193.2 47.5 %copy.46 = f32[64,1280,1,128]{3,2,0,1:T(1,128)} copy(f32[64,1280,1,128]{3,1,0,2:T(8,128)} %bitcast.53) | data formatting | bytes 83886080 | tf_op jit(solution)/shard_map/stack | solution.py:92
  240.7 26.4 %convolution_subtract_fusion = f32[64,10,128,128]{3,2,1,0:T(8,128)} fusion(f32[64,10,128,128]{3,2,1,0:T(8,128)} %fusion.29, bf16[2,64,4,10,128]{4,2,3,1,0:T(4,128)(2,1)S(1)} %get-tuple-element.18, bf16[2,64,4,10,128]{4,2,3,1,0:T(4,128)(2,1)S(1)} %get-tuple-element.17), kind=kOutput, calls=%fused_computation.6 | convolution fusion | flops 94371840 | bytes 85196800 | tf_op jit(solution)/shard_map/fspu,fspv->fpuv/dot_general | solution.py:89
  267.1 47.5 %copy.47 = f32[64,1280,1,128]{3,2,0,1:T(1,128)} copy(f32[64,1280,1,128]{3,1,0,2:T(8,128)} %bitcast.52) | data formatting | bytes 83886080 | tf_op jit(solution)/shard_map/stack | solution.py:92
  314.7 85.3 %fusion = bf16[64,1280,2,128]{3,2,0,1:T(2,128)(2,1)} fusion(f32[64,1280,1,128]{3,2,0,1:T(1,128)} %copy.47, f32[64,1280,1,128]{3,2,0,1:T(1,128)} %copy.46), kind=kLoop, calls=%fused_computation.3 | loop fusion | flops 62914560 | bytes 125829120 | tf_op jit(solution)/shard_map/convert_element_type | solution.py:92
  400.0 6.7 all-to-all-start.1
  406.7 6.5 cosine_convert_fusion.1
  413.2 895.4 %all-to-all-done.1 = bf16[64,1280,2,128]{3,2,0,1:T(2,128)(2,1)} async-done(((bf16[64,1280,2,128]{3,2,0,1:T(2,128)(2,1)}), bf16[64,1280,2,128]{3,2,0,1:T(2,128)(2,1)}, u32[]{:S(2)}, u32[]{:S(2)}) %all-to-all-start.1) | async-done | bytes 41943072 | tf_op jit(solution)/shard_map/all_to_all | solution.py:96
  1308.6 28.4 %copy.48 = bf16[64,1280,2,128]{3,1,2,0:T(8,128)(2,1)} copy(bf16[64,1280,2,128]{3,2,0,1:T(2,128)(2,1)} %all-to-all-done.1) | data formatting | bytes 83886080 | tf_op jit(solution)/shard_map/all_to_all | solution.py:96
  1336.9 29.1 %copy.49 = bf16[16,64,80,2,128]{4,2,3,1,0:T(8,128)(2,1)} copy(bf16[16,64,80,2,128]{4,2,0,3,1:T(8,128)(2,1)} %bitcast.54) | data formatting | bytes 83886080 | tf_op jit(solution)/shard_map/all_to_all | solution.py:96
  1366.1 0.0 copy-start.1
  1366.1 49.1 %bitcast_multiply_fusion = f32[80,128,384]{2,1,0:T(8,128)} fusion(bf16[1024,80,2,128]{3,1,2,0:T(8,128)(2,1)} %bitcast.55, bf16[1024,1,384]{2,0,1:T(8,128)(2,1)S(1)} %get-tuple-element.12, bf16[1024,1,384]{2,0,1:T(8,128)(2,1)S(1)} %get-tuple-element.11), kind=kOutput, calls=%fused_computation.8 | convolution fusion | flops 16110845952 | bytes 59244544 | tf_op jit(solution)/shard_map/dot_general | solution.py:95
  1415.2 0.0 copy-done.1
  (7 shorter events, 0.0 us)
Async XLA Ops:
  0.6 9.1 copy-start
  16.3 6.6 copy-start.3
  16.3 98.8 %all-to-all-start = ((f32[2,1024,1,512]{3,0,2,1:T(2,128)}), f32[2,1024,1,512]{3,0,2,1:T(2,128)}, u32[]{:S(2)}, u32[]{:S(2)}) async-start(f32[2,1024,1,512]{3,0,2,1:T(2,128)} %copy.38), calls=%async_computation | async-start | bytes 8388608 | tf_op jit(solution)/shard_map/all_to_all | solution.py:66
  120.4 5.9 collective-permute-start
  122.5 5.1 collective-permute-start.1
  127.7 0.7 copy-start.2
  400.0 908.6 %all-to-all-start.1 = ((bf16[64,1280,2,128]{3,2,0,1:T(2,128)(2,1)}), bf16[64,1280,2,128]{3,2,0,1:T(2,128)(2,1)}, u32[]{:S(2)}, u32[]{:S(2)}) async-start(bf16[64,1280,2,128]{3,2,0,1:T(2,128)(2,1)} %fusion), calls=%async_computation.1 | async-start | bytes 83886080 | tf_op jit(solution)/shard_map/all_to_all | solution.py:96
  1366.1 49.1 %copy-start.1 = (bf16[512,512]{1,0:T(8,128)(2,1)S(1)}, bf16[512,512]{1,0:T(8,128)(2,1)}, u32[]{:S(2)}) copy-start(bf16[512,512]{1,0:T(8,128)(2,1)} %param.4) | copy-start | bytes 1572868
where the time goes:
time: 1420 us
  waiting for transfers between devices  989 us (70%)
  local copies, waits for them, and re-layouts  164 us (12%)
  matrix products  133 us (9%)
  other arithmetic  110 us (8%)
  starting transfers between devices  18.2 us (1%)
    all_to_all x1, waiting for transfers between devices, per_device(): lax.all_to_all(cross_spec, 'tm', split_axis=1, concat_axis=0, tiled=True)  895 us
    another operation x2, local copies, waits for them, and re-layouts, per_device(): jnp.stack([real_part, imag_part], axis=3) / float(seg_count)  95 us
    all_to_all x1, waiting for transfers between devices, per_device(): lax.all_to_all(partial_value.reshape(2, NBIN, 1, channels), 'tm', split_a...  92.1 us
    convert_element_type x1, other arithmetic, per_device(): (jnp.stack([real_part, imag_part], axis=3) / float(seg_count)).astype(jnp...  85.3 us
    all_to_all x2, local copies, waits for them, and re-layouts, per_device(): lax.all_to_all(cross_spec, 'tm', split_axis=1, concat_axis=0, tiled=True)  57.5 us
    dot_general x1, matrix products, per_device(): lax.dot_general(lax.all_to_all(cross_spec, 'tm', split_axis=1, concat_axi...  49.1 us
  transfers between devices with their start and end apart: 4, of which 3 were waited for; matrix products, arithmetic and copies ran while one was open for 1% of the time, Pallas kernels for 0%

commit v1 on v0

v1 whole, which is shorter than its diff:
```python
import functools
import math

import jax
import jax.numpy as jnp
import numpy as np
from jax import lax
from jax.experimental import pallas as pl
from jax.experimental.pallas import tpu as pltpu
from jax.sharding import PartitionSpec as P

NBIN = 1024
SEG = 2048
GROUP = 4
BLK = 128
SMOOTH = 8
LAGS = 384
HALF = SEG // 2
HBIN = NBIN // 2
KCH = 256
MIB = 1024 * 1024

BIN_ORDER = np.concatenate([np.arange(0, NBIN, 2), np.arange(1, NBIN, 2)])


def forward_constant():
    times = np.arange(HALF)[:, None]
    parts = []
    for bins in (BIN_ORDER[:HBIN], BIN_ORDER[HBIN:]):
        phases = (times * bins[None, :] % SEG) * (2.0 * math.pi / SEG)
        parts.append(np.concatenate([np.cos(phases), -np.sin(phases)], axis=1))
    return np.stack(parts).astype(jnp.bfloat16)


def inverse_constant():
    lag_offsets = np.arange(LAGS) - LAGS // 2
    phases = (BIN_ORDER[:, None] * lag_offsets[None, :] % SEG) * (2.0 * math.pi / SEG)
    return np.stack([np.cos(phases), -np.sin(phases)]).astype(jnp.bfloat16)


def band_constant():
    return (np.abs(BIN_ORDER[:, None] - BIN_ORDER[None, :]) <= SMOOTH).astype(jnp.bfloat16)


def whiten_kernel(seg_count, per_step, x_ref, f_ref, band_ref, w_ref, amp_ref, spec, column, inv_amp):
    step = pl.program_id(1)
    rounds = seg_count // per_step

    @pl.when(step < rounds)
    def _():
        sums, diffs = [], []
        for s in range(per_step):
            first = x_ref[s * SEG : s * SEG + HALF, :].astype(jnp.float32)
            second = x_ref[s * SEG + HALF : (s + 1) * SEG, :].astype(jnp.float32)
            sums.append((first + second).astype(jnp.bfloat16).T)
            diffs.append((first - second).astype(jnp.bfloat16).T)
        total = [None, None]
        for i, folded in enumerate((sums, diffs)):
            rows = jnp.concatenate(folded, axis=0)
            for half in range(2):
                q = HBIN // 2
                cols = slice(half * q, (half + 1) * q)
                scale = 1.0 / math.sqrt(SEG)
                re = jnp.dot(rows, f_ref[i, :, half * q : (half + 1) * q], preferred_element_type=jnp.float32) * scale
                im = (
                    jnp.dot(
                        rows,
                        f_ref[i, :, HBIN + half * q : HBIN + (half + 1) * q],
                        preferred_element_type=jnp.float32,
                    )
                    * scale
                )
                magnitude = jnp.sqrt(re * re + im * im)
                at = i * HBIN + half * q
                col = jnp.zeros((BLK, q), jnp.float32)
                for s in range(per_step):
                    piece = slice(s * BLK, (s + 1) * BLK)
                    spec[step * per_step + s, 0, :, at : at + q] = re[piece]
                    spec[step * per_step + s, 1, :, at : at + q] = im[piece]
                    col = col + magnitude[piece]

                @pl.when(step == 0)
                def _():
                    column[:, at : at + q] = col

                @pl.when(step > 0)
                def _():
                    column[:, at : at + q] += col

    @pl.when(step == rounds)
    def _():
        col = column[...]
        high = col.astype(jnp.bfloat16)
        low = (col - high.astype(jnp.float32)).astype(jnp.bfloat16)
        window = jnp.dot(high, band_ref[...], preferred_element_type=jnp.float32) + jnp.dot(
            low, band_ref[...], preferred_element_type=jnp.float32
        )
        amp = window * (1.0 / float((2 * SMOOTH + 1) * seg_count)) + 1e-06
        amp_ref[...] = amp
        inv_amp[...] = 1.0 / amp

    @pl.when(step >= rounds)
    def _():
        for s in range(per_step):
            for c in range(2):
                w_ref[2 * s + c] = (spec[(step - rounds) * per_step + s, c] * inv_amp[...]).astype(jnp.bfloat16)


def whiten(samples, seg_count):
    per_step = min(seg_count, 4)
    rounds = seg_count // per_step
    channels = samples.shape[1]
    return pl.pallas_call(
        functools.partial(whiten_kernel, seg_count, per_step),
        grid=(channels // BLK, 2 * rounds),
        in_specs=[
            pl.BlockSpec((per_step * SEG, BLK), lambda h, s: (jnp.minimum(s, rounds - 1), h)),
            pl.BlockSpec((2, HALF, NBIN), lambda h, s: (0, 0, 0)),
            pl.BlockSpec((NBIN, NBIN), lambda h, s: (0, 0)),
        ],
        out_specs=[
            pl.BlockSpec((2 * per_step, BLK, NBIN), lambda h, s: (jnp.maximum(s - rounds, 0), h, 0)),
            pl.BlockSpec((BLK, NBIN), lambda h, s: (h, 0)),
        ],
        out_shape=[
            jax.ShapeDtypeStruct((2 * seg_count, channels, NBIN), jnp.bfloat16),
            jax.ShapeDtypeStruct((channels, NBIN), jnp.float32),
        ],
        scratch_shapes=[
            pltpu.VMEM((seg_count, 2, BLK, NBIN), jnp.float32),
            pltpu.VMEM((BLK, NBIN), jnp.float32),
            pltpu.VMEM((BLK, NBIN), jnp.float32),
        ],
        compiler_params=pltpu.CompilerParams(vmem_limit_bytes=60 * MIB),
    )(samples, jnp.asarray(forward_constant()), jnp.asarray(band_constant()))


def cross_terms(u_ref, v_ref, row, segs, base, k0):
    re = im = None
    for s in range(segs):
        at = base + 2 * s
        u0 = u_ref[0, at, pl.ds(row, 1), k0 : k0 + KCH]
        u1 = u_ref[0, at + 1, pl.ds(row, 1), k0 : k0 + KCH]
        u0 = jnp.broadcast_to(u0, (16, KCH)).astype(jnp.bfloat16)[None]
        u1 = jnp.broadcast_to(u1, (16, KCH)).astype(jnp.bfloat16)[None]
        v0 = v_ref[at, :, k0 : k0 + KCH].reshape(BLK // 16, 16, KCH)
        v1 = v_ref[at + 1, :, k0 : k0 + KCH].reshape(BLK // 16, 16, KCH)
        r = u0 * v0 + u1 * v1
        i = u1 * v0 - u0 * v1
        re = r if re is None else re + r
        im = i if im is None else im + i
    return re.reshape(BLK, KCH), im.reshape(BLK, KCH)


def lags_kernel(seg_count, together, unit, blocks_ref, u_ref, v_ref, inv_ref, out_ref):
    scale = 1.0 / (seg_count * math.sqrt(NBIN))

    def body(g, carry):
        acc = jnp.zeros((together * BLK, LAGS), jnp.float32)
        for k0 in range(0, NBIN, KCH):
            res, ims = [], []
            for q in range(together):
                row = g * together + q
                if seg_count <= 4:
                    re, im = cross_terms(u_ref, v_ref, row, seg_count, 0, k0)
                else:

                    def more(j, held):
                        re, im = cross_terms(u_ref, v_ref, row, 4, j * 8, k0)
                        return held[0] + re.astype(jnp.float32), held[1] + im.astype(jnp.float32)

                    zero = jnp.zeros((BLK, KCH), jnp.float32)
                    re, im = lax.fori_loop(0, seg_count // 4, more, (zero, zero))
                    re, im = re.astype(jnp.bfloat16), im.astype(jnp.bfloat16)
                res.append(re)
                ims.append(im)
            acc = acc + jnp.dot(
                jnp.concatenate(res, axis=0), inv_ref[0, k0 : k0 + KCH, :], preferred_element_type=jnp.float32
            )
            acc = acc + jnp.dot(
                jnp.concatenate(ims, axis=0), inv_ref[1, k0 : k0 + KCH, :], preferred_element_type=jnp.float32
            )
        for q in range(together):
            out_ref[g * together + q] = acc[q * BLK : (q + 1) * BLK] * scale
        return carry

    lax.fori_loop(0, unit // together, body, 0)


def lags(whitened, left_rows, right_blocks, seg_count):
    groups, _, unit, _ = left_rows.shape
    together = 2 if unit % 2 == 0 else 1
    return pl.pallas_call(
        functools.partial(lags_kernel, seg_count, together, unit),
        grid_spec=pltpu.PrefetchScalarGridSpec(
            num_scalar_prefetch=1,
            grid=(groups,),
            in_specs=[
                pl.BlockSpec((1, 2 * seg_count, unit, NBIN), lambda g, blocks: (g, 0, 0, 0)),
                pl.BlockSpec((2 * seg_count, BLK, NBIN), lambda g, blocks: (0, blocks[g], 0)),
                pl.BlockSpec((2, NBIN, LAGS), lambda g, blocks: (0, 0, 0)),
            ],
            out_specs=pl.BlockSpec((unit, BLK, LAGS), lambda g, blocks: (g, 0, 0)),
        ),
        out_shape=jax.ShapeDtypeStruct((groups * unit, BLK, LAGS), jnp.float32),
        compiler_params=pltpu.CompilerParams(vmem_limit_bytes=60 * MIB),
    )(right_blocks, left_rows, whitened, jnp.asarray(inverse_constant()))


def per_device(samples, block_pairs):
    devices = lax.axis_size("tm")
    position = lax.axis_index("tm")
    shard_len, channels = samples.shape
    seg_count = devices * shard_len // SEG
    bin_count = NBIN // devices
    rows = block_pairs.shape[0] * BLK // devices
    gathered = lax.all_gather(samples, "tm", axis=0, tiled=True)
    whitened, amp = whiten(gathered, seg_count)

    unit = math.gcd(rows, BLK)
    starts = position * rows + unit * jnp.arange(rows // unit, dtype=jnp.int32)
    pair = starts // BLK
    left_starts = block_pairs[pair, 0] * BLK + starts % BLK
    right_blocks = block_pairs[pair, 1]
    left_rows = jnp.stack(
        [
            lax.dynamic_slice_in_dim(whitened, left_starts[g], unit, axis=1).astype(jnp.float32)
            for g in range(rows // unit)
        ]
    )
    lag_values = lags(whitened, left_rows, right_blocks, seg_count)

    half = bin_count // 2
    even = lax.dynamic_slice_in_dim(amp, position * half, half, axis=1)
    odd = lax.dynamic_slice_in_dim(amp, HBIN + position * half, half, axis=1)
    amplitude = jnp.stack([even.T, odd.T], axis=1).reshape(bin_count, channels)
    return (lag_values, amplitude)


def solution(mesh):
    placed = (P(("win", "tm"), None), P())
    return jax.shard_map(
        per_device,
        mesh=mesh,
        in_specs=placed,
        out_specs=(P(("win", "tm"), None, None), P(("win", "tm"), None)),
        check_vma=False,
    )
```

time: 1420 us -> 173 us (0.12)
  the two profiles are of different devices: /device:TPU:19 before, /device:TPU:0 now
where the time goes in v1:
time: 173 us; the launch traced here: 172 us
  waiting for transfers between devices  68.3 us (39%)
  Pallas kernels  68.1 us (39%)
  between operations  23.8 us (14%)
  local copies, waits for them, and re-layouts  10.1 us (6%)
  other arithmetic  1.96 us (1%)
    all_gather x1, waiting for transfers between devices, per_device(): gathered = lax.all_gather(samples, 'tm', axis=0, tiled=True)  67.6 us
    pallas_call x1, Pallas kernels, lags(): pl.pallas_call(functools.partial(lags_kernel, seg_count, together, unit),...  43.7 us
    pallas_call x1, Pallas kernels, whiten(): pl.pallas_call(functools.partial(whiten_kernel, seg_count, per_step), gri...  24.4 us
    unnamed x6, local copies, waits for them, and re-layouts  4.33 us
  transfers between devices with their start and end apart: 1, of which 1 were waited for; matrix products, arithmetic and copies ran while one was open for 1% of the time, Pallas kernels for 0%

profile of v1, /device:TPU:0, one launch (start us, length us, event | category | flops | bytes accessed | tf_op | source)
XLA Modules:
  0.0 172.3 jit_solution(7882534233764111962)
XLA Ops:
  7.2 0.0 copy-start
  7.2 0.0 all-gather.2.cloned.1.call-start
  7.2 0.7 all-gather.2.cloned.1.call-update
  7.9 0.0 copy-done
  8.0 0.7 gather_fusion.1
  8.7 0.7 fusion.5
  15.8 1.2 gather_fusion
  20.2 67.6 %all-gather.2.cloned.1.call-done.x_ref = bf16[8192,512]{1,0:T(8,128)(2,1)} async-done(((bf16[512,512]{1,0:T(8,128)(2,1)}), bf16[8192,512]{1,0:T(8,128)(2,1)}) %all-gather.2.cloned.1.call-update) | async-done | bytes 8388624 | tf_op jit(solution)/shard_map/all_gather | solution.py:217
  87.8 24.4 %shard_map.68 = (bf16[8,512,1024]{2,1,0:T(8,128)(2,1)}, f32[512,1024]{1,0:T(8,128)}) custom-call(bf16[8192,512]{1,0:T(8,128)(2,1)} %all-gather.2.cloned.1.call-done.x_ref, bf16[2,1024,1024]{2,1,0:T(8,128)(2,1)} %constant.57.clone.f_ref, bf16[1024,1024]{1,0:T(8,128)(2,1)} %constant.58.clone.band_ref), custom_call_target="tpu_custom_call" | custom-call | tf_op jit(solution)/shard_map/pallas_call | solution.py:113
  112.2 1.2 dynamic-slice_bitcast_fusion.1
  113.4 0.2 copy.11
  113.6 0.7 reshape.71
  114.4 1.1 bitcast_dynamic-update-slice_fusion.4
  115.5 1.1 bitcast_dynamic-update-slice_fusion.3
  116.5 1.1 bitcast_dynamic-update-slice_fusion.2
  117.6 1.1 bitcast_dynamic-update-slice_fusion.1
  118.7 1.1 bitcast_dynamic-update-slice_fusion
  119.8 1.9 %stack.40.u_ref = f32[5,8,16,1024]{3,2,1,0:T(8,128)} convert(bf16[5,8,16,1024]{3,2,1,0:T(8,128)(2,1)S(1)} %bitcast_dynamic-update-slice_fusion) | non-fusion elementwise | flops 655360 | bytes 3932160 | tf_op jit(solution)/shard_map/stack | solution.py:225
  121.7 43.7 %shard_map.69 = f32[80,128,384]{2,1,0:T(8,128)} custom-call(s32[5]{0:T(128)} %gather_fusion, f32[5,8,16,1024]{3,2,1,0:T(8,128)} %stack.40.u_ref, bf16[8,512,1024]{2,1,0:T(8,128)(2,1)} %get-tuple-element.4.v_ref, bf16[2,1024,384]{2,1,0:T(8,128)(2,1)} %constant.59.clone.inv_ref), custom_call_target="tpu_custom_call" | custom-call | tf_op jit(solution)/shard_map/pallas_call | solution.py:193
  (4 shorter events, 0.1 us)
Async XLA Ops:
  7.2 0.8 copy-start
  7.2 80.6 %all-gather.2.cloned.1.call-start = ((), (), s32[]{:S(2)}) async-start(), calls=%async_computation | async-start | bytes 8912896 | tf_op jit(solution)/shard_map/all_gather | solution.py:217
Sparse Core Ops, SparseCore 0:
  10.2 77.5 all-gather.1

commit v2 on v1

--- a/solution.py
+++ b/solution.py
@@ -40,6 +40,108 @@
 
 def band_constant():
     return (np.abs(BIN_ORDER[:, None] - BIN_ORDER[None, :]) <= SMOOTH).astype(jnp.bfloat16)
+
+
+def gather_kernel(layers, x_ref, out_ref, local_sem, send_sem, recv_sem):
+    me = lax.axis_index("tm")
+    core = lax.rem(me, 2)
+    y = lax.rem(lax.div(me, 2), 2)
+    z = lax.div(me, 4)
+    length = x_ref.shape[0]
+    above, below, across, sibling = me + 4, me - 4, me + 2 - 4 * y, me + 1 - 2 * core
+    has_above, has_below = z < layers - 1, z > 0
+
+    def slot_of(layer, row, lane):
+        return layer * 4 + row * 2 + lane
+
+    def part(slot):
+        return out_ref.at[pl.ds(pl.multiple_of(slot * length, length), length), :]
+
+    def copy(kind, slot, target, src=None):
+        return pltpu.make_async_remote_copy(
+            src_ref=part(slot) if src is None else src,
+            dst_ref=part(slot),
+            send_sem=send_sem.at[kind, slot],
+            recv_sem=recv_sem.at[slot],
+            device_id={"tm": target},
+            device_id_type=pl.DeviceIdType.MESH,
+        )
+
+    def greet(target):
+        pl.semaphore_signal(
+            barrier, inc=1, device_id={"tm": target}, device_id_type=pl.DeviceIdType.MESH
+        )
+
+    barrier = pltpu.get_barrier_semaphore()
+    greet(across)
+    greet(sibling)
+    pl.when(has_above)(lambda: greet(above))
+    pl.when(has_below)(lambda: greet(below))
+    pl.semaphore_wait(barrier, 2 + jnp.minimum(z, 1) + jnp.minimum(layers - 1 - z, 1))
+
+    own = pltpu.make_async_copy(x_ref, part(me), local_sem)
+    pl.when(has_above)(lambda: copy(0, me, above, x_ref).start())
+    pl.when(has_below)(lambda: copy(1, me, below, x_ref).start())
+    copy(2, me, across, x_ref).start()
+    copy(3, me, sibling, x_ref).start()
+    own.start()
+
+    def from_across(layer):
+        slot = slot_of(layer, 1 - y, core)
+        copy(3, slot, sibling).wait_recv()
+        copy(3, slot, sibling).start()
+
+    for d in range(1, layers + 1):
+        if d < layers:
+
+            @pl.when(z - d >= 0)
+            def _():
+                slot = slot_of(z - d, y, core)
+                copy(0, slot, sibling).wait_recv()
+                pl.when(has_above)(lambda: copy(0, slot, above).start())
+                copy(2, slot, across).start()
+                copy(3, slot, sibling).start()
+
+            @pl.when(z + d < layers)
+            def _():
+                slot = slot_of(z + d, y, core)
+                copy(1, slot, sibling).wait_recv()
+                pl.when(has_below)(lambda: copy(1, slot, below).start())
+                copy(2, slot, across).start()
+                copy(3, slot, sibling).start()
+
+        pl.when(z - (d - 1) >= 0)(lambda: from_across(z - (d - 1)))
+        if d > 1:
+            pl.when(z + d - 1 < layers)(lambda: from_across(z + d - 1))
+
+    for layer in range(layers):
+        for row in range(2):
+            copy(3, slot_of(layer, row, 1 - core), sibling).wait_recv()
+    own.wait()
+    for layer in range(layers):
+        slot = slot_of(layer, y, core)
+        pl.when(jnp.logical_and(has_above, layer <= z))(lambda: copy(0, slot, above).wait_send())
+        pl.when(jnp.logical_and(has_below, layer >= z))(lambda: copy(1, slot, below).wait_send())
+        copy(2, slot, across).wait_send()
+        copy(3, slot, sibling).wait_send()
+        copy(3, slot_of(layer, 1 - y, core), sibling).wait_send()
+
+
+def gather(samples, devices):
+    if devices != 16:
+        return lax.all_gather(samples, "tm", axis=0, tiled=True)
+    return pl.pallas_call(
+        functools.partial(gather_kernel, devices // 4),
+        in_specs=[pl.BlockSpec(memory_space=pl.ANY)],
+        out_specs=pl.BlockSpec(memory_space=pl.ANY),
+        out_shape=jax.ShapeDtypeStruct((devices * samples.shape[0], samples.shape[1]), samples.dtype),
+        scratch_shapes=[
+            pltpu.SemaphoreType.DMA,
+            pltpu.SemaphoreType.DMA((4, devices)),
+            pltpu.SemaphoreType.DMA((devices,)),
+        ],
+        compiler_params=pltpu.CompilerParams(collective_id=0, has_side_effects=True),
+    )(samples)
 
 
 def whiten_kernel(seg_count, per_step, x_ref, f_ref, band_ref, w_ref, amp_ref, spec, column, inv_amp):
@@ -139,8 +241,8 @@
     re = im = None
     for s in range(segs):
         at = base + 2 * s
-        u0 = u_ref[0, at, pl.ds(row, 1), k0 : k0 + KCH]
-        u1 = u_ref[0, at + 1, pl.ds(row, 1), k0 : k0 + KCH]
+        u0 = u_ref[at, pl.ds(row, 1), k0 : k0 + KCH]
+        u1 = u_ref[at + 1, pl.ds(row, 1), k0 : k0 + KCH]
         u0 = jnp.broadcast_to(u0, (16, KCH)).astype(jnp.bfloat16)[None]
         u1 = jnp.broadcast_to(u1, (16, KCH)).astype(jnp.bfloat16)[None]
         v0 = v_ref[at, :, k0 : k0 + KCH].reshape(BLK // 16, 16, KCH)
@@ -152,8 +254,9 @@
     return re.reshape(BLK, KCH), im.reshape(BLK, KCH)
 
 
-def lags_kernel(seg_count, together, unit, blocks_ref, u_ref, v_ref, inv_ref, out_ref):
+def lags_kernel(seg_count, together, unit, lefts_ref, blocks_ref, left_ref, v_ref, inv_ref, out_ref, u_ref):
     scale = 1.0 / (seg_count * math.sqrt(NBIN))
+    u_ref[...] = left_ref[...].astype(jnp.float32)
 
     def body(g, carry):
         acc = jnp.zeros((together * BLK, LAGS), jnp.float32)
@@ -187,24 +290,30 @@
     lax.fori_loop(0, unit // together, body, 0)
 
 
-def lags(whitened, left_rows, right_blocks, seg_count):
-    groups, _, unit, _ = left_rows.shape
+def lags(whitened, left_rows, left_units, right_blocks, seg_count, unit):
+    groups = right_blocks.shape[0]
     together = 2 if unit % 2 == 0 else 1
+    if left_rows is None:
+        left_rows = whitened
+        left_spec = pl.BlockSpec((2 * seg_count, unit, NBIN), lambda g, lefts, blocks: (0, lefts[g], 0))
+    else:
+        left_spec = pl.BlockSpec((None, 2 * seg_count, unit, NBIN), lambda g, lefts, blocks: (g, 0, 0, 0))
     return pl.pallas_call(
         functools.partial(lags_kernel, seg_count, together, unit),
         grid_spec=pltpu.PrefetchScalarGridSpec(
-            num_scalar_prefetch=1,
+            num_scalar_prefetch=2,
             grid=(groups,),
             in_specs=[
-                pl.BlockSpec((1, 2 * seg_count, unit, NBIN), lambda g, blocks: (g, 0, 0, 0)),
-                pl.BlockSpec((2 * seg_count, BLK, NBIN), lambda g, blocks: (0, blocks[g], 0)),
-                pl.BlockSpec((2, NBIN, LAGS), lambda g, blocks: (0, 0, 0)),
+                left_spec,
+                pl.BlockSpec((2 * seg_count, BLK, NBIN), lambda g, lefts, blocks: (0, blocks[g], 0)),
+                pl.BlockSpec((2, NBIN, LAGS), lambda g, lefts, blocks: (0, 0, 0)),
             ],
-            out_specs=pl.BlockSpec((unit, BLK, LAGS), lambda g, blocks: (g, 0, 0)),
+            out_specs=pl.BlockSpec((unit, BLK, LAGS), lambda g, lefts, blocks: (g, 0, 0)),
+            scratch_shapes=[pltpu.VMEM((2 * seg_count, unit, NBIN), jnp.float32)],
         ),
         out_shape=jax.ShapeDtypeStruct((groups * unit, BLK, LAGS), jnp.float32),
         compiler_params=pltpu.CompilerParams(vmem_limit_bytes=60 * MIB),
-    )(right_blocks, left_rows, whitened, jnp.asarray(inverse_constant()))
+    )(left_units, right_blocks, left_rows, whitened, jnp.asarray(inverse_constant()))
 
 
 def per_device(samples, block_pairs):
@@ -214,7 +323,7 @@
     seg_count = devices * shard_len // SEG
     bin_count = NBIN // devices
     rows = block_pairs.shape[0] * BLK // devices
-    gathered = lax.all_gather(samples, "tm", axis=0, tiled=True)
+    gathered = gather(samples, devices)
     whitened, amp = whiten(gathered, seg_count)
 
     unit = math.gcd(rows, BLK)
@@ -222,13 +331,15 @@
     pair = starts // BLK
     left_starts = block_pairs[pair, 0] * BLK + starts % BLK
     right_blocks = block_pairs[pair, 1]
-    left_rows = jnp.stack(
-        [
-            lax.dynamic_slice_in_dim(whitened, left_starts[g], unit, axis=1).astype(jnp.float32)
-            for g in range(rows // unit)
-        ]
-    )
-    lag_values = lags(whitened, left_rows, right_blocks, seg_count)
+    left_rows = None
+    if unit % 16:
+        left_rows = jnp.stack(
+            [
+                lax.dynamic_slice_in_dim(whitened, left_starts[g], unit, axis=1)
+                for g in range(rows // unit)
+            ]
+        )
+    lag_values = lags(whitened, left_rows, left_starts // unit, right_blocks, seg_count, unit)
 
     half = bin_count // 2
     even = lax.dynamic_slice_in_dim(amp, position * half, half, axis=1)

time: 173 us -> 130 us (0.75)
  waiting for transfers between devices: 68.3 us -> 0 us
  Pallas kernels: 68.1 us -> 124 us
  between operations: 23.8 us -> 0.67 us
  local copies, waits for them, and re-layouts: 10.1 us -> 4.7 us
    all_gather x1 -> x0, waiting for transfers between devices: 67.6 us -> none  [per_device(): gathered = lax.all_gather(samples, 'tm', axis=0, tiled=True)]
    pallas_call x0 -> x1, Pallas kernels: none -> 57 us  [gather(): pl.pallas_call(functools.partial(gather_kernel, devices // 4), in_specs=[...]
    unnamed x6 -> x2, local copies, waits for them, and re-layouts: 4.33 us -> 0.65 us
    another operation x1 -> x0, other arithmetic: 1.87 us -> none  [per_device(): jnp.stack([lax.dynamic_slice_in_dim(whitened, left_starts[g], unit, axis=...]
  transfers between devices with their start and end apart: 1 -> 0, of which waited for: 1 -> 0; matrix products, arithmetic and copies ran while one was open for 1% -> 0% of each run, Pallas kernels for 0% -> 0%
where the time goes in v2:
time: 130 us
  Pallas kernels  124 us (95%)
  local copies, waits for them, and re-layouts  4.7 us (4%)
    pallas_call x1, Pallas kernels, gather(): pl.pallas_call(functools.partial(gather_kernel, devices // 4), in_specs=[...  57 us
    pallas_call x1, Pallas kernels, lags(): pl.pallas_call(functools.partial(lags_kernel, seg_count, together, unit),...  42.7 us
    pallas_call x1, Pallas kernels, whiten(): pl.pallas_call(functools.partial(whiten_kernel, seg_count, per_step), gri...  24.3 us

profile of v2, /device:TPU:0, one launch (start us, length us, event | category | flops | bytes accessed | tf_op | source)
XLA Modules:
  0.0 130.0 jit_solution(1337726588076096060)
XLA Ops:
  0.6 0.0 copy-start
  0.7 0.6 copy-done
  1.3 1.2 gather_fusion.1
  2.5 0.7 gather_fusion
  3.2 0.6 and_select_fusion.lefts_ref
  3.8 57.0 %shard_map.68.x_ref = bf16[8192,512]{1,0:T(8,128)(2,1)} custom-call(bf16[512,512]{1,0:T(8,128)(2,1)} %x_ref.1), custom_call_target="tpu_custom_call" | custom-call | tf_op jit(solution)/shard_map/pallas_call | solution.py:133
  60.7 24.3 %shard_map.69 = (bf16[8,512,1024]{2,1,0:T(8,128)(2,1)}, f32[512,1024]{1,0:T(8,128)}) custom-call(bf16[8192,512]{1,0:T(8,128)(2,1)} %shard_map.68.x_ref, bf16[2,1024,1024]{2,1,0:T(8,128)(2,1)} %constant.68.clone.f_ref, bf16[1024,1024]{1,0:T(8,128)(2,1)} %constant.69.clone.band_ref), custom_call_target="tpu_custom_call" | custom-call | tf_op jit(solution)/shard_map/pallas_call | solution.py:215
  85.0 1.2 dynamic-slice_bitcast_fusion.1
  86.3 0.2 copy.11
  86.5 0.7 reshape.71
  87.2 42.7 %shard_map.70 = f32[80,128,384]{2,1,0:T(8,128)} custom-call(s32[5]{0:T(128)} %and_select_fusion.lefts_ref, s32[5]{0:T(128)} %gather_fusion.1, bf16[8,512,1024]{2,1,0:T(8,128)(2,1)} %get-tuple-element.4.left_ref.v_ref, bf16[8,512,1024]{2,1,0:T(8,128)(2,1)} %get-tuple-element.4.left_ref.v_ref, bf16[2,1024,384]{2,1,0:T(8,128)(2,1)} %constant.70.clone.inv_ref), custom_call_target="tpu_custom_call" | custom-call | tf_op jit(solution)/shard_map/pallas_call | solution.py:301
  (2 shorter events, 0.1 us)
Async XLA Ops:
  0.6 0.7 copy-start

commit v3 on v2

--- a/solution.py
+++ b/solution.py
@@ -18,6 +18,8 @@
 HALF = SEG // 2
 HBIN = NBIN // 2
 KCH = 256
+PIECES = 2
+CHANS = 256
 MIB = 1024 * 1024
 
 BIN_ORDER = np.concatenate([np.arange(0, NBIN, 2), np.arange(1, NBIN, 2)])
@@ -48,21 +50,22 @@
     y = lax.rem(lax.div(me, 2), 2)
     z = lax.div(me, 4)
     length = x_ref.shape[0]
+    height = length // PIECES
     above, below, across, sibling = me + 4, me - 4, me + 2 - 4 * y, me + 1 - 2 * core
     has_above, has_below = z < layers - 1, z > 0
 
     def slot_of(layer, row, lane):
         return layer * 4 + row * 2 + lane
 
-    def part(slot):
-        return out_ref.at[pl.ds(pl.multiple_of(slot * length, length), length), :]
-
-    def copy(kind, slot, target, src=None):
+    def part(slot, piece):
+        return out_ref.at[pl.ds(pl.multiple_of(slot * length + piece * height, height), height), :]
+
+    def copy(kind, slot, piece, target, own=False):
         return pltpu.make_async_remote_copy(
-            src_ref=part(slot) if src is None else src,
-            dst_ref=part(slot),
-            send_sem=send_sem.at[kind, slot],
-            recv_sem=recv_sem.at[slot],
+            src_ref=x_ref.at[pl.ds(piece * height, height), :] if own else part(slot, piece),
+            dst_ref=part(slot, piece),
+            send_sem=send_sem.at[kind, slot, piece],
+            recv_sem=recv_sem.at[slot, piece],
             device_id={"tm": target},
             device_id_type=pl.DeviceIdType.MESH,
         )
@@ -79,52 +82,56 @@
     pl.when(has_below)(lambda: greet(below))
     pl.semaphore_wait(barrier, 2 + jnp.minimum(z, 1) + jnp.minimum(layers - 1 - z, 1))
 
-    own = pltpu.make_async_copy(x_ref, part(me), local_sem)
-    pl.when(has_above)(lambda: copy(0, me, above, x_ref).start())
-    pl.when(has_below)(lambda: copy(1, me, below, x_ref).start())
-    copy(2, me, across, x_ref).start()
-    copy(3, me, sibling, x_ref).start()
+    for piece in range(PIECES):
+        pl.when(has_above)(lambda: copy(0, me, piece, above, True).start())
+        pl.when(has_below)(lambda: copy(1, me, piece, below, True).start())
+        copy(2, me, piece, across, True).start()
+        copy(3, me, piece, sibling, True).start()
+    own = pltpu.make_async_copy(x_ref, out_ref.at[pl.ds(pl.multiple_of(me * length, length), length), :], local_sem)
     own.start()
 
-    def from_across(layer):
+    def from_across(layer, piece):
         slot = slot_of(layer, 1 - y, core)
-        copy(3, slot, sibling).wait_recv()
-        copy(3, slot, sibling).start()
+        copy(3, slot, piece, sibling).wait_recv()
+        copy(3, slot, piece, sibling).start()
 
     for d in range(1, layers + 1):
-        if d < layers:
-
-            @pl.when(z - d >= 0)
-            def _():
-                slot = slot_of(z - d, y, core)
-                copy(0, slot, sibling).wait_recv()
-                pl.when(has_above)(lambda: copy(0, slot, above).start())
-                copy(2, slot, across).start()
-                copy(3, slot, sibling).start()
-
-            @pl.when(z + d < layers)
-            def _():
-                slot = slot_of(z + d, y, core)
-                copy(1, slot, sibling).wait_recv()
-                pl.when(has_below)(lambda: copy(1, slot, below).start())
-                copy(2, slot, across).start()
-                copy(3, slot, sibling).start()
-
-        pl.when(z - (d - 1) >= 0)(lambda: from_across(z - (d - 1)))
-        if d > 1:
-            pl.when(z + d - 1 < layers)(lambda: from_across(z + d - 1))
+        for piece in range(PIECES):
+            if d < layers:
+
+                @pl.when(z - d >= 0)
+                def _():
+                    slot = slot_of(z - d, y, core)
+                    copy(0, slot, piece, sibling).wait_recv()
+                    pl.when(has_above)(lambda: copy(0, slot, piece, above).start())
+                    copy(2, slot, piece, across).start()
+                    copy(3, slot, piece, sibling).start()
+
+                @pl.when(z + d < layers)
+                def _():
+                    slot = slot_of(z + d, y, core)
+                    copy(1, slot, piece, sibling).wait_recv()
+                    pl.when(has_below)(lambda: copy(1, slot, piece, below).start())
+                    copy(2, slot, piece, across).start()
+                    copy(3, slot, piece, sibling).start()
+
+            pl.when(z - (d - 1) >= 0)(lambda: from_across(z - (d - 1), piece))
+            if d > 1:
+                pl.when(z + d - 1 < layers)(lambda: from_across(z + d - 1, piece))
 
     for layer in range(layers):
         for row in range(2):
-            copy(3, slot_of(layer, row, 1 - core), sibling).wait_recv()
+            for piece in range(PIECES):
+                copy(3, slot_of(layer, row, 1 - core), piece, sibling).wait_recv()
     own.wait()
     for layer in range(layers):
         slot = slot_of(layer, y, core)
-        pl.when(jnp.logical_and(has_above, layer <= z))(lambda: copy(0, slot, above).wait_send())
-        pl.when(jnp.logical_and(has_below, layer >= z))(lambda: copy(1, slot, below).wait_send())
-        copy(2, slot, across).wait_send()
-        copy(3, slot, sibling).wait_send()
-        copy(3, slot_of(layer, 1 - y, core), sibling).wait_send()
+        for piece in range(PIECES):
+            pl.when(jnp.logical_and(has_above, layer <= z))(lambda: copy(0, slot, piece, above).wait_send())
+            pl.when(jnp.logical_and(has_below, layer >= z))(lambda: copy(1, slot, piece, below).wait_send())
+            copy(2, slot, piece, across).wait_send()
+            copy(3, slot, piece, sibling).wait_send()
+            copy(3, slot_of(layer, 1 - y, core), piece, sibling).wait_send()
 
 
 def gather(samples, devices):
@@ -137,8 +144,8 @@
         out_shape=jax.ShapeDtypeStruct((devices * samples.shape[0], samples.shape[1]), samples.dtype),
         scratch_shapes=[
             pltpu.SemaphoreType.DMA,
-            pltpu.SemaphoreType.DMA((4, devices)),
-            pltpu.SemaphoreType.DMA((devices,)),
+            pltpu.SemaphoreType.DMA((4, devices, PIECES)),
+            pltpu.SemaphoreType.DMA((devices, PIECES)),
         ],
         compiler_params=pltpu.CompilerParams(collective_id=0, has_side_effects=True),
     )(samples)
@@ -147,6 +154,7 @@
 def whiten_kernel(seg_count, per_step, x_ref, f_ref, band_ref, w_ref, amp_ref, spec, column, inv_amp):
     step = pl.program_id(1)
     rounds = seg_count // per_step
+    chans = x_ref.shape[1]
 
     @pl.when(step < rounds)
     def _():
@@ -174,9 +182,9 @@
                 )
                 magnitude = jnp.sqrt(re * re + im * im)
                 at = i * HBIN + half * q
-                col = jnp.zeros((BLK, q), jnp.float32)
+                col = jnp.zeros((chans, q), jnp.float32)
                 for s in range(per_step):
-                    piece = slice(s * BLK, (s + 1) * BLK)
+                    piece = slice(s * chans, (s + 1) * chans)
                     spec[step * per_step + s, 0, :, at : at + q] = re[piece]
                     spec[step * per_step + s, 1, :, at : at + q] = im[piece]
                     col = col + magnitude[piece]
@@ -194,9 +202,10 @@
         col = column[...]
         high = col.astype(jnp.bfloat16)
         low = (col - high.astype(jnp.float32)).astype(jnp.bfloat16)
-        window = jnp.dot(high, band_ref[...], preferred_element_type=jnp.float32) + jnp.dot(
-            low, band_ref[...], preferred_element_type=jnp.float32
+        both = jnp.dot(
+            jnp.concatenate([high, low], axis=0), band_ref[...], preferred_element_type=jnp.float32
         )
+        window = both[:chans] + both[chans:]
         amp = window * (1.0 / float((2 * SMOOTH + 1) * seg_count)) + 1e-06
         amp_ref[...] = amp
         inv_amp[...] = 1.0 / amp
@@ -212,26 +221,27 @@
     per_step = min(seg_count, 4)
     rounds = seg_count // per_step
     channels = samples.shape[1]
+    chans = CHANS if rounds == 1 else BLK
     return pl.pallas_call(
         functools.partial(whiten_kernel, seg_count, per_step),
-        grid=(channels // BLK, 2 * rounds),
+        grid=(channels // chans, 2 * rounds),
         in_specs=[
-            pl.BlockSpec((per_step * SEG, BLK), lambda h, s: (jnp.minimum(s, rounds - 1), h)),
+            pl.BlockSpec((per_step * SEG, chans), lambda h, s: (jnp.minimum(s, rounds - 1), h)),
             pl.BlockSpec((2, HALF, NBIN), lambda h, s: (0, 0, 0)),
             pl.BlockSpec((NBIN, NBIN), lambda h, s: (0, 0)),
         ],
         out_specs=[
-            pl.BlockSpec((2 * per_step, BLK, NBIN), lambda h, s: (jnp.maximum(s - rounds, 0), h, 0)),
-            pl.BlockSpec((BLK, NBIN), lambda h, s: (h, 0)),
+            pl.BlockSpec((2 * per_step, chans, NBIN), lambda h, s: (jnp.maximum(s - rounds, 0), h, 0)),
+            pl.BlockSpec((chans, NBIN), lambda h, s: (h, 0)),
         ],
         out_shape=[
             jax.ShapeDtypeStruct((2 * seg_count, channels, NBIN), jnp.bfloat16),
             jax.ShapeDtypeStruct((channels, NBIN), jnp.float32),
         ],
         scratch_shapes=[
-            pltpu.VMEM((seg_count, 2, BLK, NBIN), jnp.float32),
-            pltpu.VMEM((BLK, NBIN), jnp.float32),
-            pltpu.VMEM((BLK, NBIN), jnp.float32),
+            pltpu.VMEM((seg_count, 2, chans, NBIN), jnp.float32),
+            pltpu.VMEM((chans, NBIN), jnp.float32),
+            pltpu.VMEM((chans, NBIN), jnp.float32),
         ],
         compiler_params=pltpu.CompilerParams(vmem_limit_bytes=60 * MIB),
     )(samples, jnp.asarray(forward_constant()), jnp.asarray(band_constant()))
@@ -287,12 +297,15 @@
             out_ref[g * together + q] = acc[q * BLK : (q + 1) * BLK] * scale
         return carry
 
-    lax.fori_loop(0, unit // together, body, 0)
+    if unit == together:
+        body(0, 0)
+    else:
+        lax.fori_loop(0, unit // together, body, 0)
 
 
 def lags(whitened, left_rows, left_units, right_blocks, seg_count, unit):
     groups = right_blocks.shape[0]
-    together = 2 if unit % 2 == 0 else 1
+    together = math.gcd(unit, 8)
     if left_rows is None:
         left_rows = whitened
         left_spec = pl.BlockSpec((2 * seg_count, unit, NBIN), lambda g, lefts, blocks: (0, lefts[g], 0))

time: 130 us -> 113 us (0.87)
  Pallas kernels: 124 us -> 107 us
    pallas_call x1, Pallas kernels: 42.7 us -> 30.9 us  [lags(): pl.pallas_call(functools.partial(lags_kernel, seg_count, together, unit),...]
    pallas_call x1, Pallas kernels: 57 us -> 53.2 us  [gather(): pl.pallas_call(functools.partial(gather_kernel, devices // 4), in_specs=[...]
    pallas_call x1, Pallas kernels: 24.3 us -> 22.8 us  [whiten(): pl.pallas_call(functools.partial(whiten_kernel, seg_count, per_step), gri...]
where the time goes in v3:
time: 113 us
  Pallas kernels  107 us (95%)
  local copies, waits for them, and re-layouts  4.7 us (4%)
    pallas_call x1, Pallas kernels, gather(): pl.pallas_call(functools.partial(gather_kernel, devices // 4), in_specs=[...  53.2 us
    pallas_call x1, Pallas kernels, lags(): pl.pallas_call(functools.partial(lags_kernel, seg_count, together, unit),...  30.9 us
    pallas_call x1, Pallas kernels, whiten(): pl.pallas_call(functools.partial(whiten_kernel, seg_count, per_step), gri...  22.8 us

profile of v3, /device:TPU:0, one launch (start us, length us, event | category | flops | bytes accessed | tf_op | source)
XLA Modules:
  0.0 112.9 jit_solution(12954419083934343861)
XLA Ops:
  0.6 0.0 copy-start
  0.7 0.6 copy-done
  1.3 1.2 %gather_fusion.1 = s32[5]{0:T(128)} fusion(s32[10,2]{0,1:T(2,128)S(1)} %copy-done, s32[5]{0:T(128)S(1)} %get-tuple-element.8), kind=kCustom, calls=%fused_computation.1 | custom fusion | bytes 80 | tf_op jit(solution)/shard_map/gather | solution.py:346
  2.5 0.7 gather_fusion
  3.2 0.6 and_select_fusion.lefts_ref
  3.8 53.2 %shard_map.68.x_ref = bf16[8192,512]{1,0:T(8,128)(2,1)} custom-call(bf16[512,512]{1,0:T(8,128)(2,1)} %x_ref.1), custom_call_target="tpu_custom_call" | custom-call | tf_op jit(solution)/shard_map/pallas_call | solution.py:140
  57.0 22.8 %shard_map.69 = (bf16[8,512,1024]{2,1,0:T(8,128)(2,1)}, f32[512,1024]{1,0:T(8,128)}) custom-call(bf16[8192,512]{1,0:T(8,128)(2,1)} %shard_map.68.x_ref, bf16[2,1024,1024]{2,1,0:T(8,128)(2,1)} %constant.68.clone.f_ref, bf16[1024,1024]{1,0:T(8,128)(2,1)} %constant.69.clone.band_ref), custom_call_target="tpu_custom_call" | custom-call | tf_op jit(solution)/shard_map/pallas_call | solution.py:225
  79.7 1.2 %dynamic-slice_bitcast_fusion.1 = (f32[32,1,512]{0,2,1:T(8,128)S(1)}, f32[32,1,512]{0,2,1:T(8,128)S(1)}) fusion(f32[512,1024]{1,0:T(8,128)} %get-tuple-element.5, s32[]{:T(128)S(6)} %select_n.43, s32[]{:T(128)S(6)} %select_n.44), kind=kLoop, calls=%fused_computation.4 | loop fusion | bytes 262152 | tf_op jit(solution)/shard_map/stack | solution.py:360
  81.0 0.2 copy.11
  81.2 0.7 reshape.71
  81.9 30.9 %shard_map.70 = f32[80,128,384]{2,1,0:T(8,128)} custom-call(s32[5]{0:T(128)} %and_select_fusion.lefts_ref, s32[5]{0:T(128)} %gather_fusion.1, bf16[8,512,1024]{2,1,0:T(8,128)(2,1)} %get-tuple-element.4.left_ref.v_ref, bf16[8,512,1024]{2,1,0:T(8,128)(2,1)} %get-tuple-element.4.left_ref.v_ref, bf16[2,1024,384]{2,1,0:T(8,128)(2,1)} %constant.70.clone.inv_ref), custom_call_target="tpu_custom_call" | custom-call | tf_op jit(solution)/shard_map/pallas_call | solution.py:314
  (2 shorter events, 0.1 us)
Async XLA Ops:
  0.6 0.7 copy-start

commit v4 on v3

--- a/solution.py
+++ b/solution.py
@@ -15,33 +15,26 @@
 BLK = 128
 SMOOTH = 8
 LAGS = 384
-HALF = SEG // 2
 HBIN = NBIN // 2
 KCH = 256
 PIECES = 2
 CHANS = 256
 MIB = 1024 * 1024
 
-BIN_ORDER = np.concatenate([np.arange(0, NBIN, 2), np.arange(1, NBIN, 2)])
-
 
 def forward_constant():
-    times = np.arange(HALF)[:, None]
-    parts = []
-    for bins in (BIN_ORDER[:HBIN], BIN_ORDER[HBIN:]):
-        phases = (times * bins[None, :] % SEG) * (2.0 * math.pi / SEG)
-        parts.append(np.concatenate([np.cos(phases), -np.sin(phases)], axis=1))
-    return np.stack(parts).astype(jnp.bfloat16)
+    phases = (np.arange(SEG)[:, None] * np.arange(NBIN)[None, :] % SEG) * (2.0 * math.pi / SEG)
+    return np.concatenate([np.cos(phases), -np.sin(phases)], axis=1).astype(jnp.bfloat16)
 
 
 def inverse_constant():
     lag_offsets = np.arange(LAGS) - LAGS // 2
-    phases = (BIN_ORDER[:, None] * lag_offsets[None, :] % SEG) * (2.0 * math.pi / SEG)
+    phases = (np.arange(NBIN)[:, None] * lag_offsets[None, :] % SEG) * (2.0 * math.pi / SEG)
     return np.stack([np.cos(phases), -np.sin(phases)]).astype(jnp.bfloat16)
 
 
 def band_constant():
-    return (np.abs(BIN_ORDER[:, None] - BIN_ORDER[None, :]) <= SMOOTH).astype(jnp.bfloat16)
+    return (np.abs(np.arange(NBIN)[:, None] - np.arange(NBIN)[None, :]) <= SMOOTH).astype(jnp.bfloat16)
 
 
 def gather_kernel(layers, x_ref, out_ref, local_sem, send_sem, recv_sem):
@@ -158,44 +151,27 @@
 
     @pl.when(step < rounds)
     def _():
-        sums, diffs = [], []
-        for s in range(per_step):
-            first = x_ref[s * SEG : s * SEG + HALF, :].astype(jnp.float32)
-            second = x_ref[s * SEG + HALF : (s + 1) * SEG, :].astype(jnp.float32)
-            sums.append((first + second).astype(jnp.bfloat16).T)
-            diffs.append((first - second).astype(jnp.bfloat16).T)
-        total = [None, None]
-        for i, folded in enumerate((sums, diffs)):
-            rows = jnp.concatenate(folded, axis=0)
-            for half in range(2):
-                q = HBIN // 2
-                cols = slice(half * q, (half + 1) * q)
-                scale = 1.0 / math.sqrt(SEG)
-                re = jnp.dot(rows, f_ref[i, :, half * q : (half + 1) * q], preferred_element_type=jnp.float32) * scale
-                im = (
-                    jnp.dot(
-                        rows,
-                        f_ref[i, :, HBIN + half * q : HBIN + (half + 1) * q],
-                        preferred_element_type=jnp.float32,
-                    )
-                    * scale
-                )
-                magnitude = jnp.sqrt(re * re + im * im)
-                at = i * HBIN + half * q
-                col = jnp.zeros((chans, q), jnp.float32)
-                for s in range(per_step):
-                    piece = slice(s * chans, (s + 1) * chans)
-                    spec[step * per_step + s, 0, :, at : at + q] = re[piece]
-                    spec[step * per_step + s, 1, :, at : at + q] = im[piece]
-                    col = col + magnitude[piece]
-
-                @pl.when(step == 0)
-                def _():
-                    column[:, at : at + q] = col
-
-                @pl.when(step > 0)
-                def _():
-                    column[:, at : at + q] += col
+        rows = jnp.concatenate([x_ref[s * SEG : (s + 1) * SEG, :].T for s in range(per_step)], axis=0)
+        q = HBIN
+        scale = 1.0 / math.sqrt(SEG)
+        for at in range(0, NBIN, q):
+            re = jnp.dot(rows, f_ref[:, at : at + q], preferred_element_type=jnp.float32) * scale
+            im = jnp.dot(rows, f_ref[:, NBIN + at : NBIN + at + q], preferred_element_type=jnp.float32) * scale
+            magnitude = jnp.sqrt(re * re + im * im)
+            col = jnp.zeros((chans, q), jnp.float32)
+            for s in range(per_step):
+                piece = slice(s * chans, (s + 1) * chans)
+                spec[step * per_step + s, 0, :, at : at + q] = re[piece]
+                spec[step * per_step + s, 1, :, at : at + q] = im[piece]
+                col = col + magnitude[piece]
+
+            @pl.when(step == 0)
+            def _():
+                column[:, at : at + q] = col
+
+            @pl.when(step > 0)
+            def _():
+                column[:, at : at + q] += col
 
     @pl.when(step == rounds)
     def _():
@@ -227,7 +203,7 @@
         grid=(channels // chans, 2 * rounds),
         in_specs=[
             pl.BlockSpec((per_step * SEG, chans), lambda h, s: (jnp.minimum(s, rounds - 1), h)),
-            pl.BlockSpec((2, HALF, NBIN), lambda h, s: (0, 0, 0)),
+            pl.BlockSpec((SEG, 2 * NBIN), lambda h, s: (0, 0), pipeline_mode=pl.Buffered(1)),
             pl.BlockSpec((NBIN, NBIN), lambda h, s: (0, 0)),
         ],
         out_specs=[
@@ -354,10 +330,7 @@
         )
     lag_values = lags(whitened, left_rows, left_starts // unit, right_blocks, seg_count, unit)
 
-    half = bin_count // 2
-    even = lax.dynamic_slice_in_dim(amp, position * half, half, axis=1)
-    odd = lax.dynamic_slice_in_dim(amp, HBIN + position * half, half, axis=1)
-    amplitude = jnp.stack([even.T, odd.T], axis=1).reshape(bin_count, channels)
+    amplitude = lax.dynamic_slice_in_dim(amp, position * bin_count, bin_count, axis=1).T
     return (lag_values, amplitude)
 
 

time: 113 us -> 122 us (1.080)
  Pallas kernels: 107 us -> 116 us
    pallas_call x1, Pallas kernels: 22.8 us -> 32.3 us  [whiten(): pl.pallas_call(functools.partial(whiten_kernel, seg_count, per_step), gri...]
    another operation x2 -> x0, local copies, waits for them, and re-layouts: 1.42 us -> none  [per_device(): amplitude = jnp.stack([even.T, odd.T], axis=1).reshape(bin_count, channels)]
where the time goes in v4:
time: 122 us
  Pallas kernels  116 us (95%)
  local copies, waits for them, and re-layouts  4.37 us (4%)
    pallas_call x1, Pallas kernels, gather(): pl.pallas_call(functools.partial(gather_kernel, devices // 4), in_specs=[...  53.2 us
    pallas_call x1, Pallas kernels, whiten(): pl.pallas_call(functools.partial(whiten_kernel, seg_count, per_step), gri...  32.3 us
    pallas_call x1, Pallas kernels, lags(): pl.pallas_call(functools.partial(lags_kernel, seg_count, together, unit),...  30.9 us

profile of v4, /device:TPU:0, one launch (start us, length us, event | category | flops | bytes accessed | tf_op | source)
XLA Modules:
  0.0 122.0 jit_solution(16713862126021733265)
XLA Ops:
  0.6 0.0 copy-start
  0.7 0.6 copy-done
  1.3 1.2 gather_fusion.1
  2.5 0.7 gather_fusion
  3.2 0.6 and_select_fusion.lefts_ref
  3.8 53.2 %shard_map.68.x_ref = bf16[8192,512]{1,0:T(8,128)(2,1)} custom-call(bf16[512,512]{1,0:T(8,128)(2,1)} %x_ref.1), custom_call_target="tpu_custom_call" | custom-call | tf_op jit(solution)/shard_map/pallas_call | solution.py:133
  57.0 32.3 %shard_map.69 = (bf16[8,512,1024]{2,1,0:T(8,128)(2,1)}, f32[512,1024]{1,0:T(8,128)}) custom-call(bf16[8192,512]{1,0:T(8,128)(2,1)} %shard_map.68.x_ref, bf16[2048,2048]{1,0:T(8,128)(2,1)} %constant.64.clone.f_ref, bf16[1024,1024]{1,0:T(8,128)(2,1)} %constant.65.clone.band_ref), custom_call_target="tpu_custom_call" | custom-call | tf_op jit(solution)/shard_map/pallas_call | solution.py:201
  89.3 1.1 dynamic-slice_bitcast_fusion
  90.3 0.8 copy.8
  91.1 30.9 %shard_map.70 = f32[80,128,384]{2,1,0:T(8,128)} custom-call(s32[5]{0:T(128)} %and_select_fusion.lefts_ref, s32[5]{0:T(128)} %gather_fusion.1, bf16[8,512,1024]{2,1,0:T(8,128)(2,1)} %get-tuple-element.4.left_ref.v_ref, bf16[8,512,1024]{2,1,0:T(8,128)(2,1)} %get-tuple-element.4.left_ref.v_ref, bf16[2,1024,384]{2,1,0:T(8,128)(2,1)} %constant.66.clone.inv_ref), custom_call_target="tpu_custom_call" | custom-call | tf_op jit(solution)/shard_map/pallas_call | solution.py:290
  (1 shorter events, 0.0 us)
Async XLA Ops:
  0.6 0.7 copy-start
